TPU v7x, 32 devices: a whole 2x2x4 slice. The times are simulated.
32 devices in a mesh: groups: 2 (over y), seq: 16 (over z, x, core).
Axes of the slice: x: 2, y: 2, z: 4, core: 2. Of those that a mesh axis runs over, the one named last changes fastest.
Arguments:
- q_fresh: bfloat16 [2048, 5120], P(('groups', 'seq')), parts along dimension 0, may hold values from -48 to 48
- k_fresh: bfloat16 [2048, 5120], P(('groups', 'seq')), parts along dimension 0, may hold values from -48 to 48
- v_fresh: bfloat16 [2048, 5120], P(('groups', 'seq')), parts along dimension 0, may hold values from -6 to 6
- q_gain: bfloat16 [5120], replicated, may hold values from 1 to 4
- k_gain: bfloat16 [5120], replicated, may hold values from 0.5 to 2
- stale_keys: bfloat16 [32, 512, 640], P(('groups', 'seq')), parts along dimension 0, may hold values from -6 to 6
- stale_values: bfloat16 [32, 512, 640], P(('groups', 'seq')), parts along dimension 0, may hold values from -6 to 6
- gate_table: bfloat16 [50, 5120], replicated, may hold values from 0.5 to 3
- assign: int32 [32], P('groups'), parts along dimension 0, may hold values from 0 to 15, each once
- counts: int32 [32], P('groups'), parts along dimension 0, may hold values from 1 to 64, 768 in all
- timestep: int32 [2], P('groups'), parts along dimension 0, may hold values from 0 to 49
Outputs:
- mixed: bfloat16 [2048, 5120], P(('groups', 'seq')), parts along dimension 0
- new_keys: bfloat16 [32, 512, 640], P(('groups', 'seq')), parts along dimension 0
- new_values: bfloat16 [32, 512, 640], P(('groups', 'seq')), parts along dimension 0
There are 2 independent parts, one for each index of `groups`. A program takes and returns all parts, laid end to end along the dimension named above; an argument that names none is the same for every part. Nothing has to cross between parts.
Inputs may be any that keep to these rules, and one draw needn't show every extreme that they name: Index i of seq holds the rows of patch assign[i]; every patch is held once. `counts`: some patch has all 64 tokens live.
All inputs are finite; a program needn't handle non-finite values.
Results may differ from a plain program's by a relative error of at most 0.011.
Values may be sent and summed in bfloat16 or wider, within the bound.
No kernel may reach another device: no remote copies, remote signals or barrier semaphores. Data moves between devices by JAX's collectives and lax.ppermute only.
A program may use at most 64 MiB of HBM per device.

v0:
```python
import functools

import jax
import jax.numpy as jnp
import numpy as np
from jax import lax
from jax.experimental import pallas as pl
from jax.experimental.pallas import tpu as pltpu
from jax.sharding import PartitionSpec as P

HEAD = 128
RMS_EPS = 1e-06
VMEM_BYTES = 32 * 1024 * 1024
TILE = 256
SMEM, VMEM = pltpu.SMEM, pltpu.VMEM


def call(kernel, name, ins, outs, flops, n_bytes, scratch=()):
    shapes = [jax.ShapeDtypeStruct(shape, dtype) for _, shape, dtype in outs]
    return pl.pallas_call(
        kernel,
        out_shape=shapes,
        in_specs=[pl.BlockSpec(memory_space=m) for m in ins],
        out_specs=[pl.BlockSpec(memory_space=m) for m, _, _ in outs],
        scratch_shapes=scratch,
        compiler_params=pltpu.CompilerParams(vmem_limit_bytes=VMEM_BYTES),
        cost_estimate=pl.CostEstimate(flops=flops, bytes_accessed=n_bytes, transcendentals=0),
        name=name,
    )


def to_partner(value, distance, size):
    if distance == 0:
        return value
    return lax.ppermute(value, "seq", [(i, i ^ distance) for i in range(size)])


def to_block(value, distance, size):
    return lax.ppermute(value, "seq", [(i, (i + distance) % size) for i in range(size)])


def column(h):
    return slice(h * HEAD, (h + 1) * HEAD)


def place(slots):
    device = lax.axis_index("seq")
    return lax.rem(device, slots), lax.div(device, slots)


def live_of(assign, counts, index):
    return counts[assign[index]]


def live_lanes(assign, counts, tok, indices):
    width = tok * len(indices)
    lane = lax.broadcasted_iota(jnp.int32, (1, width), 1)
    count = jnp.zeros((1, width), jnp.int32)
    for i, index in enumerate(indices):
        count = jnp.where(lane // tok == i, live_of(assign, counts, index), count)
    return lane % tok, count


def compact_kernel(slots, tok, blocks, assign, counts, keys, values, *refs):
    flag, outs = refs[0], refs[1:]
    wide = keys.shape[2]
    rows = slots * tok
    _, block = place(slots)
    indices = [block * slots + i for i in range(slots)]
    within, count = live_lanes(assign, counts, tok, indices)
    lane = lax.broadcasted_iota(jnp.int32, (1, rows), 1)
    ahead = jnp.zeros((1, rows), jnp.int32)
    for i, index in enumerate(indices):
        ahead = ahead + jnp.where(lane // tok > i, live_of(assign, counts, index), 0)
    goal = jnp.where(within < count, ahead + within, -1)
    row = lax.broadcasted_iota(jnp.int32, (rows, rows), 0)
    pick = jnp.where(row == goal, 1.0, 0.0).astype(jnp.bfloat16)
    most = jnp.int32(0)
    for b in range(blocks):
        total = jnp.int32(0)
        for i in range(slots):
            total = total + live_of(assign, counts, b * slots + i)
        most = jnp.maximum(most, total)
    flag[0] = most
    for part, ref in enumerate((keys, values)):
        start = 0
        for out in outs:
            stop = start + out.shape[0]
            moved = jnp.dot(pick[start:stop], ref[0], preferred_element_type=jnp.float32)
            out[:, part * wide : (part + 1) * wide] = moved.astype(jnp.bfloat16)
            start = stop


def norm_kernel(order, heads, assign, q, k, v, q_gain, k_gain, steps, *outs):
    tok, width = q.shape
    slot, block = place(len(order))
    patch = assign[block * len(order) + slot]
    position = patch * tok + lax.broadcasted_iota(jnp.int32, (tok, HEAD), 0)
    angles = position.astype(jnp.float32) * steps[...]
    low = lax.broadcasted_iota(jnp.int32, (tok, HEAD), 1) < HEAD // 2
    cos_part = jnp.cos(angles)
    sin_part = jnp.sin(angles)
    sin_part = jnp.where(low, -sin_part, sin_part)

    def inverse(ref):
        total = jnp.zeros((tok, HEAD), jnp.float32)
        for c in range(0, width, HEAD):
            x = ref[:, c : c + HEAD].astype(jnp.float32)
            total = total + x * x
        return lax.rsqrt(jnp.sum(total, axis=1, keepdims=True) / width + RMS_EPS)

    scales = inverse(q), inverse(k)
    for out, d in zip(outs, order):
        group = jnp.bitwise_xor(slot, d)
        for h in range(heads):
            col = pl.ds(pl.multiple_of((group * heads + h) * HEAD, HEAD), HEAD)
            for part, (ref, gain) in enumerate(((q, q_gain), (k, k_gain))):
                x = ref[:, col].astype(jnp.float32) * scales[part]
                x = x * gain[:, col].astype(jnp.float32)
                turned = x * cos_part + pltpu.roll(x, HEAD // 2, 1) * sin_part
                out[part * tok : (part + 1) * tok, column(h)] = turned.astype(jnp.bfloat16)
            out[2 * tok : 3 * tok, column(h)] = v[:, col]


def cache_kernel(order, tok, *refs):
    new_keys, new_values = refs[len(order) :]
    slot, _ = place(len(order))
    for ref, d in zip(refs, order):
        at = pl.ds(pl.multiple_of(jnp.bitwise_xor(slot, d) * tok, tok), tok)
        new_keys[0, at, :] = ref[tok : 2 * tok, :]
        new_values[0, at, :] = ref[2 * tok : 3 * tok, :]


def softmax_step(queries, keys, values, bias, state):
    scale = HEAD**-0.5
    scores = lax.dot_general(
        queries, keys, (((1,), (1,)), ((), ())), preferred_element_type=jnp.float32
    )
    scores = scores + bias
    top = jnp.max(scores, axis=1, keepdims=True)
    if state is not None:
        top = jnp.maximum(top, state[0])
    weights = jnp.exp((scores - top) * scale)
    total = jnp.sum(weights, axis=1, keepdims=True)
    summed = jnp.dot(weights.astype(jnp.bfloat16), values, preferred_element_type=jnp.float32)
    if state is not None:
        fading = jnp.exp((state[0] - top) * scale)
        total = total + state[1] * fading
        summed = summed + state[2] * fading
    return top, total, summed


def store_state(stats, sums, at, parts):
    rows = parts[0][0].shape[0]
    lane = lax.broadcasted_iota(jnp.int32, (rows, HEAD), 1)
    packed = jnp.zeros((rows, HEAD), jnp.float32)
    for h, (top, total, summed) in enumerate(parts):
        packed = jnp.where(lane == h, top, packed)
        packed = jnp.where(lane == HEAD // 2 + h, total, packed)
        sums[at, column(h)] = summed
    stats[at, :] = packed


def load_state(stats, sums, at, h):
    half = HEAD // 2
    return stats[at, h : h + 1], stats[at, half + h : half + h + 1], sums[at, column(h)]


def fresh_kernel(order, tok, heads, assign, counts, *refs):
    slots = len(order)
    bundles = refs[:slots]
    queries, stats, sums, keys, values = refs[slots:]
    for i, bundle in enumerate(bundles):
        at = slice(i * tok, (i + 1) * tok)
        queries[at, :] = bundle[:tok, :]
        keys[at, :] = bundle[tok : 2 * tok, :]
        values[at, :] = bundle[2 * tok : 3 * tok, :]
    slot, block = place(slots)
    indices = [block * slots + jnp.bitwise_xor(slot, d) for d in order]
    within, count = live_lanes(assign, counts, tok, indices)
    bias = jnp.where(within < count, 0.0, -jnp.inf)
    for start in range(0, slots * tok, TILE):
        at = slice(start, start + TILE)
        parts = []
        for h in range(heads):
            cols = column(h)
            parts.append(
                softmax_step(queries[at, cols], keys[:, cols], values[:, cols], bias, None)
            )
        store_state(stats, sums, at, parts)


def stale_kernel(slots, tok, blocks, step, heads, rows, final, assign, counts, *refs):
    queries, stats, sums = refs[:3]
    pieces = refs[3 : 3 + final[0]]
    rest = refs[3 + final[0] :]
    _, block = place(slots)
    source = lax.rem(block - step + blocks, blocks) * slots
    live = jnp.int32(0)
    for i in range(slots):
        live = live + live_of(assign, counts, source + i)
    width = sum(p.shape[0] for p in pieces)
    lane = lax.broadcasted_iota(jnp.int32, (1, width), 1)
    bias = jnp.where(lane < live, 0.0, -jnp.inf)

    def joined(cols):
        if len(pieces) == 1:
            return pieces[0][:, cols]
        return jnp.concatenate([p[:, cols] for p in pieces], axis=0)

    for start in range(*rows, TILE):
        at = slice(start, start + TILE)
        parts = []
        for h in range(heads):
            parts.append(
                softmax_step(
                    queries[at, column(h)],
                    joined(column(h)),
                    joined(column(heads + h)),
                    bias,
                    load_state(stats, sums, at, h),
                )
            )
        if not final[1]:
            store_state(*rest, at, parts)
            continue
        gate, outs = rest[0], rest[1:]
        for h, (_, total, summed) in enumerate(parts):
            out = (summed / total).astype(jnp.bfloat16).astype(jnp.float32)
            out = (out * gate[:, column(h)].astype(jnp.float32)).astype(jnp.bfloat16)
            for i in range(TILE // tok):
                to = (start - rows[0]) // tok + i
                outs[to][:, column(h)] = out[i * tok : (i + 1) * tok]


def collect_kernel(order, heads, *refs):
    wide = heads * HEAD
    slot, _ = place(len(order))
    for ref, d in zip(refs, order):
        group = jnp.bitwise_xor(slot, d)
        refs[-1][:, pl.ds(pl.multiple_of(group * wide, wide), wide)] = ref[...]


def body(
    q_fresh,
    k_fresh,
    v_fresh,
    q_gain,
    k_gain,
    stale_keys,
    stale_values,
    gate_table,
    assign,
    counts,
    timestep,
):
    bf16, f32, i32 = jnp.bfloat16, jnp.float32, jnp.int32
    device = lax.axis_index("seq")
    size = lax.axis_size("seq")
    tok, model_width = q_fresh.shape
    block_rows, wide = stale_keys.shape[1:]
    slots = model_width // wide
    blocks = size // slots
    heads = wide // HEAD
    order = sorted(range(slots), key=lambda d: (-(d & ~1).bit_count(), -d))
    short = block_rows * 7 // 8 if blocks == 2 else block_rows
    sizes = [n for n in (short, block_rows - short) if n]

    most, *packed = call(
        functools.partial(compact_kernel, slots, tok, blocks),
        "compact",
        [SMEM, SMEM, VMEM, VMEM],
        [(SMEM, (1,), i32)] + [(VMEM, (n, 2 * wide), bf16) for n in sizes],
        4 * block_rows * block_rows * wide,
        8 * block_rows * wide,
    )(assign, counts, stale_keys, stale_values)

    def exchange(arrays, order):
        return [to_partner(a, d, size) for a, d in zip(arrays, order)]

    halves = np.arange(HEAD, dtype=np.float64) % (HEAD // 2)
    steps = jnp.asarray((10000.0 ** (-2.0 * halves / HEAD)).astype(np.float32)[None])

    def run(packed, operands):
        assign, counts, q, k, v, q_gain, k_gain, gate_table, timestep = operands
        stale = [[to_block(p, s * slots, size) for p in packed] for s in range(1, blocks)]
        bundles = call(
            functools.partial(norm_kernel, order, heads),
            "norm",
            [SMEM] + [VMEM] * 6,
            [(VMEM, (3 * tok, wide), bf16)] * slots,
            20 * tok * model_width,
            12 * tok * model_width,
        )(assign, q, k, v, q_gain[None], k_gain[None], steps)
        fresh = exchange(bundles, order)
        gate = lax.dynamic_slice(gate_table, (timestep[0], device % slots * wide), (1, wide))
        state_like = [(VMEM, (block_rows, HEAD), f32), (VMEM, (block_rows, wide), f32)]
        queries, *state = call(
            functools.partial(fresh_kernel, order, tok, heads),
            "fresh",
            [SMEM] * 2 + [VMEM] * slots,
            [(VMEM, (block_rows, wide), bf16), *state_like],
            4 * block_rows * block_rows * wide,
            16 * block_rows * wide,
            [pltpu.VMEM((block_rows, wide), bf16)] * 2,
        )(assign, counts, *fresh)

        def step(s, rows, outs, extra):
            final = (len(packed), s == blocks - 1)
            return call(
                functools.partial(stale_kernel, slots, tok, blocks, s, heads, rows, final),
                "stale",
                [SMEM] * 2 + [VMEM] * (3 + len(packed) + len(extra)),
                outs,
                4 * (rows[1] - rows[0]) * block_rows * wide,
                8 * block_rows * wide,
            )(assign, counts, queries, *state, *stale[s - 1], *extra)

        for s in range(1, blocks - 1):
            state = step(s, (0, block_rows), state_like, [])
        back = []
        for start in range(0, block_rows, TILE):
            part = order[start // tok : (start + TILE) // tok]
            outs = [(VMEM, (tok, wide), bf16)] * len(part)
            back += exchange(step(blocks - 1, (start, start + TILE), outs, [gate]), part)
        new_keys, new_values = call(
            functools.partial(cache_kernel, order, tok),
            "cache",
            [VMEM] * slots,
            [(VMEM, (1, block_rows, wide), bf16)] * 2,
            0,
            8 * block_rows * wide,
        )(*fresh)
        (mixed,) = call(
            functools.partial(collect_kernel, order, heads),
            "collect",
            [VMEM] * slots,
            [(VMEM, (tok, model_width), bf16)],
            0,
            4 * tok * model_width,
        )(*back)
        return mixed, new_keys, new_values

    operands = (
        assign,
        counts,
        q_fresh,
        k_fresh,
        v_fresh,
        q_gain,
        k_gain,
        gate_table,
        timestep,
    )
    if len(sizes) == 1:
        return run(packed, operands)
    return lax.cond(
        most[0] <= sizes[0],
        lambda packed, operands: run(packed[:1], operands),
        run,
        packed,
        operands,
    )


def solution(mesh):
    rows = P(("groups", "seq"), None)
    entries = P(("groups", "seq"), None, None)
    return jax.shard_map(
        body,
        mesh=mesh,
        in_specs=(
            rows,
            rows,
            rows,
            P(),
            P(),
            entries,
            entries,
            P(),
            P("groups"),
            P("groups"),
            P("groups"),
        ),
        out_specs=(rows, entries, entries),
        check_vma=False,
    )
```

profile of v0, /device:TPU:0, one launch (start us, length us, event | category | flops | bytes accessed | tf_op | source)
XLA Modules:
  0.0 83.8 jit_solution(5846720186178967339)
XLA Ops:
  0.6 1.1 %copy-done = bf16[1,512,640]{2,1,0:T(8,128)(2,1)S(1)} copy-done((bf16[1,512,640]{2,1,0:T(8,128)(2,1)S(1)}, bf16[1,512,640]{2,1,0:T(8,128)(2,1)}, u32[]{:S(2)}) %copy-start) | copy-done | bytes 655384
  1.7 1.1 %copy-done.1 = bf16[1,512,640]{2,1,0:T(8,128)(2,1)S(1)} copy-done((bf16[1,512,640]{2,1,0:T(8,128)(2,1)S(1)}, bf16[1,512,640]{2,1,0:T(8,128)(2,1)}, u32[]{:S(2)}) %copy-start.1) | copy-done | bytes 655384
  2.8 0.0 copy-start.9
  2.9 3.0 %compact.1 = (s32[1]{0:T(128)}, bf16[448,1280]{1,0:T(8,128)(2,1)}, bf16[64,1280]{1,0:T(8,128)(2,1)}) custom-call(s32[16]{0:T(128)} %assign.1, s32[16]{0:T(128)} %counts.1, bf16[1,512,640]{2,1,0:T(8,128)(2,1)S(1)} %copy-done, bf16[1,512,640]{2,1,0:T(8,128)(2,1)S(1)} %copy-done.1), custom_call_target="tpu_custom_call" | custom-call | flops 671088640 | bytes 2621440 | tf_op jit(solution)/shard_map/compact/pallas_call | solution.py:269
  6.6 76.3 %conditional.1 = (bf16[1,512,640]{2,1,0:T(8,128)(2,1)}, bf16[1,512,640]{2,1,0:T(8,128)(2,1)}, bf16[64,5120]{1,0:T(8,128)(2,1)S(1)}) conditional(s32[]{:T(128)} %bitcast.2, (bf16[5120]{0:T(1024)(128)(2,1)S(1)}, bf16[5120]{0:T(1024)(128)(2,1)S(1)}, s32[16]{0:T(128)S(1)}, bf16[64,5120]{1,0:T(8,128)(2,1)S(1)}, bf16[64,5120]{1,0:T(8,128)(2,1)S(1)}, ...), branch_computations={%region_0.1_spmd, %region_1.2_spmd} | conditional | flops 1348730880 | bytes 32812368 | solution.py:357
  6.8 4.1 %collective-permute-start.23 = (bf16[448,1280]{1,0:T(8,128)(2,1)}, bf16[448,1280]{1,0:T(8,128)(2,1)S(1)}, u32[]{:S(2)}, u32[]{:S(2)}) collective-permute-start(bf16[448,1280]{1,0:T(8,128)(2,1)} %get-tuple-element.103), channel_id=1, source_target_pairs={{0,8},{1,9},{2,10},{3,11},{4,12},{5,13},{6,14},{7,15},{8,0},{9,1},... | collective-permute-start | bytes 3440648 | tf_op jit(solution)/shard_map/cond/branch_1_fun/ppermute | solution.py:39
  11.0 3.0 %norm.3 = (bf16[192,640]{1,0:T(8,128)(2,1)S(1)}, bf16[192,640]{1,0:T(8,128)(2,1)S(1)}, bf16[192,640]{1,0:T(8,128)(2,1)S(1)}, bf16[192,640]{1,0:T(8,128)(2,1)}, b...) custom-call(s32[16]{0:T(128)S(1)} %get-tuple-element.84.assign, ...), custom_call_target="tpu_custom_call" | custom-call | flops 6553600 | bytes 3932160 | tf_op jit(solution)/shard_map/cond/branch_1_fun/norm/pallas_call | solution.py:287
  14.0 1.7 %collective-permute-start.16 = (bf16[192,640]{1,0:T(8,128)(2,1)S(1)}, bf16[192,640]{1,0:T(8,128)(2,1)S(1)}, u32[]{:S(2)}, u32[]{:S(2)}) collective-permute-start(bf16[192,640]{1,0:T(8,128)(2,1)S(1)} %get-tuple-element.92), channel_id=1, source_target_pairs={{0,7},{1,6},{2,5},{3,4},{4,3},{5,2},{6,1},{7,0},{8,15},{9,14},{10,... | collective-permute-start | bytes 737288 | tf_op jit(solution)/shard_map/cond/branch_1_fun/ppermute | solution.py:35
  15.6 0.9 %collective-permute-start.17 = (bf16[192,640]{1,0:T(8,128)(2,1)S(1)}, bf16[192,640]{1,0:T(8,128)(2,1)S(1)}, u32[]{:S(2)}, u32[]{:S(2)}) collective-permute-start(bf16[192,640]{1,0:T(8,128)(2,1)S(1)} %get-tuple-element.93), channel_id=1, source_target_pairs={{0,6},{1,7},{2,4},{3,5},{4,2},{5,3},{6,0},{7,1},{8,14},{9,15},{10,... | collective-permute-start | bytes 737288 | tf_op jit(solution)/shard_map/cond/branch_1_fun/ppermute | solution.py:35
  16.5 1.4 %collective-permute-start.18 = (bf16[192,640]{1,0:T(8,128)(2,1)S(1)}, bf16[192,640]{1,0:T(8,128)(2,1)S(1)}, u32[]{:S(2)}, u32[]{:S(2)}) collective-permute-start(bf16[192,640]{1,0:T(8,128)(2,1)S(1)} %get-tuple-element.94), channel_id=1, source_target_pairs={{0,5},{1,4},{2,7},{3,6},{4,1},{5,0},{6,3},{7,2},{8,13},{9,12},{10,... | collective-permute-start | bytes 737288 | tf_op jit(solution)/shard_map/cond/branch_1_fun/ppermute | solution.py:35
  17.9 0.4 collective-permute-start.19
  18.4 23.7 %collective-permute-done.16.refs_0_ = bf16[192,640]{1,0:T(8,128)(2,1)S(1)} collective-permute-done((bf16[192,640]{1,0:T(8,128)(2,1)S(1)}, bf16[192,640]{1,0:T(8,128)(2,1)S(1)}, u32[]{:S(2)}, u32[]{:S(2)}) %collective-permute-start.16) | collective-permute-done | bytes 245792 | tf_op jit(solution)/shard_map/cond/branch_1_fun/ppermute | solution.py:35
  42.1 5.3 %collective-permute-done.17.refs_1_ = bf16[192,640]{1,0:T(8,128)(2,1)S(1)} collective-permute-done((bf16[192,640]{1,0:T(8,128)(2,1)S(1)}, bf16[192,640]{1,0:T(8,128)(2,1)S(1)}, u32[]{:S(2)}, u32[]{:S(2)}) %collective-permute-start.17) | collective-permute-done | bytes 245792 | tf_op jit(solution)/shard_map/cond/branch_1_fun/ppermute | solution.py:35
  47.4 1.5 %collective-permute-start.21 = (bf16[192,640]{1,0:T(8,128)(2,1)}, bf16[192,640]{1,0:T(8,128)(2,1)S(1)}, u32[]{:S(2)}, u32[]{:S(2)}) collective-permute-start(bf16[192,640]{1,0:T(8,128)(2,1)} %get-tuple-element.97), channel_id=1, source_target_pairs={{0,2},{1,3},{2,0},{3,1},{4,6},{5,7},{6,4},{7,5},{8,10},{9,11},{10,... | collective-permute-start | bytes 737288 | tf_op jit(solution)/shard_map/cond/branch_1_fun/ppermute | solution.py:35
  48.9 3.8 %collective-permute-done.18.refs_2_ = bf16[192,640]{1,0:T(8,128)(2,1)S(1)} collective-permute-done((bf16[192,640]{1,0:T(8,128)(2,1)S(1)}, bf16[192,640]{1,0:T(8,128)(2,1)S(1)}, u32[]{:S(2)}, u32[]{:S(2)}) %collective-permute-start.18) | collective-permute-done | bytes 245792 | tf_op jit(solution)/shard_map/cond/branch_1_fun/ppermute | solution.py:35
  54.6 0.8 dynamic_slice.5.refs_4_
  55.4 6.5 %collective-permute-done.19.refs_3_ = bf16[192,640]{1,0:T(8,128)(2,1)S(1)} collective-permute-done((bf16[192,640]{1,0:T(8,128)(2,1)}, bf16[192,640]{1,0:T(8,128)(2,1)S(1)}, u32[]{:S(2)}, u32[]{:S(2)}) %collective-permute-start.19) | collective-permute-done | bytes 245792 | tf_op jit(solution)/shard_map/cond/branch_1_fun/ppermute | solution.py:35
  61.8 3.9 %fresh.3 = (bf16[512,640]{1,0:T(8,128)(2,1)S(1)}, f32[512,128]{1,0:T(8,128)S(1)}, f32[512,640]{1,0:T(8,128)S(1)}) custom-call(s32[16]{0:T(128)S(1)} %get-tuple-element.84.assign, s32[16]{0:T(128)S(1)} %get-tuple-element.85.counts, bf16[192,640]{1,0:T(8,128)(2,1)S(1)} %collective-permute-done.16.refs_0_, ...), custom_call_target="tpu_custom_call" | custom-call | flops 671088640 | bytes 5242880 | tf_op jit(solution)/shard_map/cond/branch_1_fun/fresh/pallas_call | solution.py:298
  65.8 3.0 %stale.6 = (bf16[64,640]{1,0:T(8,128)(2,1)S(1)}, bf16[64,640]{1,0:T(8,128)(2,1)S(1)}, bf16[64,640]{1,0:T(8,128)(2,1)S(1)}, bf16[64,640]{1,0:T(8,128)(2,1)S(1)}) custom-call(s32[16]{0:T(128)S(1)} %get-tuple-element.84.assign, s32[16]{0:T(128)S(1)} %get-tuple-element.85.counts, bf16[512,640]{1,0:T(8,128)(2,1)S(1)} %get-tuple-element.100.refs_0_, ...), custom_call_target="tpu_custom_call" | custom-call | flops 335544320 | bytes 2621440 | tf_op jit(solution)/shard_map/cond/branch_1_fun/stale/pallas_call | solution.py:310
  68.8 0.1 collective-permute-start.24
  68.9 2.6 %collective-permute-start.25 = (bf16[64,640]{1,0:T(8,128)(2,1)S(1)}, bf16[64,640]{1,0:T(8,128)(2,1)S(1)}, u32[]{:S(2)}, u32[]{:S(2)}) collective-permute-start(bf16[64,640]{1,0:T(8,128)(2,1)S(1)} %get-tuple-element.108), channel_id=1, source_target_pairs={{0,6},{1,7},{2,4},{3,5},{4,2},{5,3},{6,0},{7,1},{8,14},{9,15},{10,... | collective-permute-start | bytes 245768 | tf_op jit(solution)/shard_map/cond/branch_1_fun/ppermute | solution.py:35
  71.5 1.8 %collective-permute-start.27 = (bf16[64,640]{1,0:T(8,128)(2,1)S(1)}, bf16[64,640]{1,0:T(8,128)(2,1)S(1)}, u32[]{:S(2)}, u32[]{:S(2)}) collective-permute-start(bf16[64,640]{1,0:T(8,128)(2,1)S(1)} %get-tuple-element.110), channel_id=1, source_target_pairs={{0,4},{1,5},{2,6},{3,7},{4,0},{5,1},{6,2},{7,3},{8,12},{9,13},{10,... | collective-permute-start | bytes 245768 | tf_op jit(solution)/shard_map/cond/branch_1_fun/ppermute | solution.py:35
  73.3 3.0 %stale.7 = (bf16[64,640]{1,0:T(8,128)(2,1)S(1)}, bf16[64,640]{1,0:T(8,128)(2,1)S(1)}, bf16[64,640]{1,0:T(8,128)(2,1)S(1)}, bf16[64,640]{1,0:T(8,128)(2,1)S(1)}) custom-call(s32[16]{0:T(128)S(1)} %get-tuple-element.84.assign, s32[16]{0:T(128)S(1)} %get-tuple-element.85.counts, bf16[512,640]{1,0:T(8,128)(2,1)S(1)} %get-tuple-element.100.refs_0_, ...), custom_call_target="tpu_custom_call" | custom-call | flops 335544320 | bytes 2621440 | tf_op jit(solution)/shard_map/cond/branch_1_fun/stale/pallas_call | solution.py:310
  76.3 0.7 collective-permute-start.28
  77.0 1.1 %collective-permute-start.29 = (bf16[64,640]{1,0:T(8,128)(2,1)S(1)}, bf16[64,640]{1,0:T(8,128)(2,1)S(1)}, u32[]{:S(2)}, u32[]{:S(2)}) collective-permute-start(bf16[64,640]{1,0:T(8,128)(2,1)S(1)} %get-tuple-element.112), channel_id=1, source_target_pairs={{0,2},{1,3},{2,0},{3,1},{4,6},{5,7},{6,4},{7,5},{8,10},{9,11},{10,... | collective-permute-start | bytes 245768 | tf_op jit(solution)/shard_map/cond/branch_1_fun/ppermute | solution.py:35
  78.0 0.2 collective-permute-start.30
  78.2 1.2 %cache.3 = (bf16[1,512,640]{2,1,0:T(8,128)(2,1)}, bf16[1,512,640]{2,1,0:T(8,128)(2,1)}) custom-call(bf16[192,640]{1,0:T(8,128)(2,1)S(1)} %collective-permute-done.16.refs_0_, bf16[192,640]{1,0:T(8,128)(2,1)S(1)} %collective-permute-done.17.refs_1_, bf16[192,640]{1,0:T(8,128)(2,1)S(1)} %collective-permute-done.18.refs_2_, ...), custom_call_target="tpu_custom_call" | custom-call | bytes 2621440 | tf_op jit(solution)/shard_map/cond/branch_1_fun/cache/pallas_call | solution.py:326
  79.4 0.0 collective-permute-done.27.refs_3_
  79.4 1.4 %collective-permute-done.28.refs_4_ = bf16[64,640]{1,0:T(8,128)(2,1)S(1)} collective-permute-done((bf16[64,640]{1,0:T(8,128)(2,1)S(1)}, bf16[64,640]{1,0:T(8,128)(2,1)S(1)}, u32[]{:S(2)}, u32[]{:S(2)}) %collective-permute-start.28) | collective-permute-done | bytes 81952 | tf_op jit(solution)/shard_map/cond/branch_1_fun/ppermute | solution.py:35
  80.8 2.0 %collective-permute-done.29.refs_5_ = bf16[64,640]{1,0:T(8,128)(2,1)S(1)} collective-permute-done((bf16[64,640]{1,0:T(8,128)(2,1)S(1)}, bf16[64,640]{1,0:T(8,128)(2,1)S(1)}, u32[]{:S(2)}, u32[]{:S(2)}) %collective-permute-start.29) | collective-permute-done | bytes 81952 | tf_op jit(solution)/shard_map/cond/branch_1_fun/ppermute | solution.py:35
  82.8 0.1 collect.3
  82.9 0.8 copy-done.4
  (31 shorter events, 0.1 us)
Async XLA Ops:
  0.6 1.1 %copy-start = (bf16[1,512,640]{2,1,0:T(8,128)(2,1)S(1)}, bf16[1,512,640]{2,1,0:T(8,128)(2,1)}, u32[]{:S(2)}) copy-start(bf16[1,512,640]{2,1,0:T(8,128)(2,1)} %keys.1) | copy-start | bytes 1966084
  1.7 1.1 %copy-start.1 = (bf16[1,512,640]{2,1,0:T(8,128)(2,1)S(1)}, bf16[1,512,640]{2,1,0:T(8,128)(2,1)}, u32[]{:S(2)}) copy-start(bf16[1,512,640]{2,1,0:T(8,128)(2,1)} %values.1) | copy-start | bytes 1966084
  2.8 3.7 %copy-start.2 = (bf16[64,5120]{1,0:T(8,128)(2,1)S(1)}, bf16[64,5120]{1,0:T(8,128)(2,1)}, u32[]{:S(2)}) copy-start(bf16[64,5120]{1,0:T(8,128)(2,1)} %param.14) | copy-start | bytes 1966084
  2.8 3.7 %copy-start.3 = (bf16[64,5120]{1,0:T(8,128)(2,1)S(1)}, bf16[64,5120]{1,0:T(8,128)(2,1)}, u32[]{:S(2)}) copy-start(bf16[64,5120]{1,0:T(8,128)(2,1)} %param.15) | copy-start | bytes 1966084
  2.8 3.7 %copy-start.5 = (bf16[5120]{0:T(1024)(128)(2,1)S(1)}, bf16[5120]{0:T(1024)(128)(2,1)}, u32[]{:S(2)}) copy-start(bf16[5120]{0:T(1024)(128)(2,1)} %param.17) | copy-start | bytes 30724
  2.8 3.7 %copy-start.6 = (bf16[5120]{0:T(1024)(128)(2,1)S(1)}, bf16[5120]{0:T(1024)(128)(2,1)}, u32[]{:S(2)}) copy-start(bf16[5120]{0:T(1024)(128)(2,1)} %param.18) | copy-start | bytes 30724
  2.8 3.7 %copy-start.7 = (s32[16]{0:T(128)S(1)}, s32[16]{0:T(128)}, u32[]{:S(2)}) copy-start(s32[16]{0:T(128)} %assign.1) | copy-start | bytes 196
  2.8 3.7 %copy-start.8 = (s32[16]{0:T(128)S(1)}, s32[16]{0:T(128)}, u32[]{:S(2)}) copy-start(s32[16]{0:T(128)} %counts.1) | copy-start | bytes 196
  2.8 3.7 %copy-start.9 = (f32[1,128]{1,0:T(1,128)S(1)}, f32[1,128]{1,0:T(1,128)}, u32[]{:S(2)}) copy-start(f32[1,128]{1,0:T(1,128)} %constant.47.clone) | copy-start | bytes 1540
  6.8 4.2 %copy-start.10 = (f32[1,128]{1,0:T(1,128)}, f32[1,128]{1,0:T(1,128)S(1)}, u32[]{:S(2)}) copy-start(f32[1,128]{1,0:T(1,128)S(1)} %get-tuple-element.91.steps) | copy-start | bytes 1540 | tf_op jit(solution)/shard_map/cond
  6.8 59.0 %collective-permute-start.23 = (bf16[448,1280]{1,0:T(8,128)(2,1)}, bf16[448,1280]{1,0:T(8,128)(2,1)S(1)}, u32[]{:S(2)}, u32[]{:S(2)}) collective-permute-start(bf16[448,1280]{1,0:T(8,128)(2,1)} %get-tuple-element.103), channel_id=1, source_target_pairs={{0,8},{1,9},{2,10},{3,11},{4,12},{5,13},{6,14},{7,15},{8,0},{9,1},... | collective-permute-start | bytes 3440648 | tf_op jit(solution)/shard_map/cond/branch_1_fun/ppermute | solution.py:39
  14.0 28.1 %collective-permute-start.16 = (bf16[192,640]{1,0:T(8,128)(2,1)S(1)}, bf16[192,640]{1,0:T(8,128)(2,1)S(1)}, u32[]{:S(2)}, u32[]{:S(2)}) collective-permute-start(bf16[192,640]{1,0:T(8,128)(2,1)S(1)} %get-tuple-element.92), channel_id=1, source_target_pairs={{0,7},{1,6},{2,5},{3,4},{4,3},{5,2},{6,1},{7,0},{8,15},{9,14},{10,... | collective-permute-start | bytes 737288 | tf_op jit(solution)/shard_map/cond/branch_1_fun/ppermute | solution.py:35
  15.6 31.7 %collective-permute-start.17 = (bf16[192,640]{1,0:T(8,128)(2,1)S(1)}, bf16[192,640]{1,0:T(8,128)(2,1)S(1)}, u32[]{:S(2)}, u32[]{:S(2)}) collective-permute-start(bf16[192,640]{1,0:T(8,128)(2,1)S(1)} %get-tuple-element.93), channel_id=1, source_target_pairs={{0,6},{1,7},{2,4},{3,5},{4,2},{5,3},{6,0},{7,1},{8,14},{9,15},{10,... | collective-permute-start | bytes 737288 | tf_op jit(solution)/shard_map/cond/branch_1_fun/ppermute | solution.py:35
  16.5 36.1 %collective-permute-start.18 = (bf16[192,640]{1,0:T(8,128)(2,1)S(1)}, bf16[192,640]{1,0:T(8,128)(2,1)S(1)}, u32[]{:S(2)}, u32[]{:S(2)}) collective-permute-start(bf16[192,640]{1,0:T(8,128)(2,1)S(1)} %get-tuple-element.94), channel_id=1, source_target_pairs={{0,5},{1,4},{2,7},{3,6},{4,1},{5,0},{6,3},{7,2},{8,13},{9,12},{10,... | collective-permute-start | bytes 737288 | tf_op jit(solution)/shard_map/cond/branch_1_fun/ppermute | solution.py:35
  17.9 43.9 %collective-permute-start.19 = (bf16[192,640]{1,0:T(8,128)(2,1)}, bf16[192,640]{1,0:T(8,128)(2,1)S(1)}, u32[]{:S(2)}, u32[]{:S(2)}) collective-permute-start(bf16[192,640]{1,0:T(8,128)(2,1)} %get-tuple-element.95), channel_id=1, source_target_pairs={{0,4},{1,5},{2,6},{3,7},{4,0},{5,1},{6,2},{7,3},{8,12},{9,13},{10,... | collective-permute-start | bytes 737288 | tf_op jit(solution)/shard_map/cond/branch_1_fun/ppermute | solution.py:35
  42.1 19.7 %collective-permute-start.20 = (bf16[192,640]{1,0:T(8,128)(2,1)}, bf16[192,640]{1,0:T(8,128)(2,1)S(1)}, u32[]{:S(2)}, u32[]{:S(2)}) collective-permute-start(bf16[192,640]{1,0:T(8,128)(2,1)} %get-tuple-element.96), channel_id=1, source_target_pairs={{0,3},{1,2},{2,1},{3,0},{4,7},{5,6},{6,5},{7,4},{8,11},{9,10},{10,... | collective-permute-start | bytes 737288 | tf_op jit(solution)/shard_map/cond/branch_1_fun/ppermute | solution.py:35
  47.4 14.5 %collective-permute-start.21 = (bf16[192,640]{1,0:T(8,128)(2,1)}, bf16[192,640]{1,0:T(8,128)(2,1)S(1)}, u32[]{:S(2)}, u32[]{:S(2)}) collective-permute-start(bf16[192,640]{1,0:T(8,128)(2,1)} %get-tuple-element.97), channel_id=1, source_target_pairs={{0,2},{1,3},{2,0},{3,1},{4,6},{5,7},{6,4},{7,5},{8,10},{9,11},{10,... | collective-permute-start | bytes 737288 | tf_op jit(solution)/shard_map/cond/branch_1_fun/ppermute | solution.py:35
  52.6 9.2 %collective-permute-start.22 = (bf16[192,640]{1,0:T(8,128)(2,1)S(1)}, bf16[192,640]{1,0:T(8,128)(2,1)S(1)}, u32[]{:S(2)}, u32[]{:S(2)}) collective-permute-start(bf16[192,640]{1,0:T(8,128)(2,1)S(1)} %get-tuple-element.98), channel_id=1, source_target_pairs={{0,1},{1,0},{2,3},{3,2},{4,5},{5,4},{6,7},{7,6},{8,9},{9,8},{10,11... | collective-permute-start | bytes 737288 | tf_op jit(solution)/shard_map/cond/branch_1_fun/ppermute | solution.py:35
  68.8 8.2 %collective-permute-start.24 = (bf16[64,640]{1,0:T(8,128)(2,1)S(1)}, bf16[64,640]{1,0:T(8,128)(2,1)S(1)}, u32[]{:S(2)}, u32[]{:S(2)}) collective-permute-start(bf16[64,640]{1,0:T(8,128)(2,1)S(1)} %get-tuple-element.107), channel_id=1, source_target_pairs={{0,7},{1,6},{2,5},{3,4},{4,3},{5,2},{6,1},{7,0},{8,15},{9,14},{10,... | collective-permute-start | bytes 245768 | tf_op jit(solution)/shard_map/cond/branch_1_fun/ppermute | solution.py:35
  68.9 9.2 %collective-permute-start.25 = (bf16[64,640]{1,0:T(8,128)(2,1)S(1)}, bf16[64,640]{1,0:T(8,128)(2,1)S(1)}, u32[]{:S(2)}, u32[]{:S(2)}) collective-permute-start(bf16[64,640]{1,0:T(8,128)(2,1)S(1)} %get-tuple-element.108), channel_id=1, source_target_pairs={{0,6},{1,7},{2,4},{3,5},{4,2},{5,3},{6,0},{7,1},{8,14},{9,15},{10,... | collective-permute-start | bytes 245768 | tf_op jit(solution)/shard_map/cond/branch_1_fun/ppermute | solution.py:35
  71.5 7.9 %collective-permute-start.26 = (bf16[64,640]{1,0:T(8,128)(2,1)S(1)}, bf16[64,640]{1,0:T(8,128)(2,1)S(1)}, u32[]{:S(2)}, u32[]{:S(2)}) collective-permute-start(bf16[64,640]{1,0:T(8,128)(2,1)S(1)} %get-tuple-element.109), channel_id=1, source_target_pairs={{0,5},{1,4},{2,7},{3,6},{4,1},{5,0},{6,3},{7,2},{8,13},{9,12},{10,... | collective-permute-start | bytes 245768 | tf_op jit(solution)/shard_map/cond/branch_1_fun/ppermute | solution.py:35
  71.5 7.9 %collective-permute-start.27 = (bf16[64,640]{1,0:T(8,128)(2,1)S(1)}, bf16[64,640]{1,0:T(8,128)(2,1)S(1)}, u32[]{:S(2)}, u32[]{:S(2)}) collective-permute-start(bf16[64,640]{1,0:T(8,128)(2,1)S(1)} %get-tuple-element.110), channel_id=1, source_target_pairs={{0,4},{1,5},{2,6},{3,7},{4,0},{5,1},{6,2},{7,3},{8,12},{9,13},{10,... | collective-permute-start | bytes 245768 | tf_op jit(solution)/shard_map/cond/branch_1_fun/ppermute | solution.py:35
  76.3 4.6 %collective-permute-start.28 = (bf16[64,640]{1,0:T(8,128)(2,1)S(1)}, bf16[64,640]{1,0:T(8,128)(2,1)S(1)}, u32[]{:S(2)}, u32[]{:S(2)}) collective-permute-start(bf16[64,640]{1,0:T(8,128)(2,1)S(1)} %get-tuple-element.111), channel_id=1, source_target_pairs={{0,3},{1,2},{2,1},{3,0},{4,7},{5,6},{6,5},{7,4},{8,11},{9,10},{10,... | collective-permute-start | bytes 245768 | tf_op jit(solution)/shard_map/cond/branch_1_fun/ppermute | solution.py:35
  77.0 5.9 %collective-permute-start.29 = (bf16[64,640]{1,0:T(8,128)(2,1)S(1)}, bf16[64,640]{1,0:T(8,128)(2,1)S(1)}, u32[]{:S(2)}, u32[]{:S(2)}) collective-permute-start(bf16[64,640]{1,0:T(8,128)(2,1)S(1)} %get-tuple-element.112), channel_id=1, source_target_pairs={{0,2},{1,3},{2,0},{3,1},{4,6},{5,7},{6,4},{7,5},{8,10},{9,11},{10,... | collective-permute-start | bytes 245768 | tf_op jit(solution)/shard_map/cond/branch_1_fun/ppermute | solution.py:35
  78.0 4.8 %collective-permute-start.30 = (bf16[64,640]{1,0:T(8,128)(2,1)S(1)}, bf16[64,640]{1,0:T(8,128)(2,1)S(1)}, u32[]{:S(2)}, u32[]{:S(2)}) collective-permute-start(bf16[64,640]{1,0:T(8,128)(2,1)S(1)} %get-tuple-element.113), channel_id=1, source_target_pairs={{0,1},{1,0},{2,3},{3,2},{4,5},{5,4},{6,7},{7,6},{8,9},{9,8},{10,11... | collective-permute-start | bytes 245768 | tf_op jit(solution)/shard_map/cond/branch_1_fun/ppermute | solution.py:35
  82.9 0.8 %copy-start.4 = (bf16[64,5120]{1,0:T(8,128)(2,1)}, bf16[64,5120]{1,0:T(8,128)(2,1)S(1)}, u32[]{:S(2)}) copy-start(bf16[64,5120]{1,0:T(8,128)(2,1)S(1)} %get-tuple-element.126) | copy-start | bytes 1966084
where the time goes:
time: 84.1 us; the launch traced here: 83.8 us
  waiting for transfers between devices  42.7 us (51%)
  Pallas kernels  17.2 us (20%)
  starting transfers between devices  16.4 us (20%)
  local copies, waits for them, and re-layouts  3.85 us (5%)
  loops' own time  2.23 us (3%)
  between operations  1.4 us (2%)
    ppermute x14, waiting for transfers between devices, to_partner(): return lax.ppermute(value, 'seq', [(i, i ^ distance) for i in range(size)])  42.7 us
    ppermute x14, starting transfers between devices, to_partner(): return lax.ppermute(value, 'seq', [(i, i ^ distance) for i in range(size)])  12.3 us
    pallas_call x2, Pallas kernels, step(): call(functools.partial(stale_kernel, slots, tok, blocks, s, heads, rows,...  5.99 us
    ppermute x1, starting transfers between devices, to_block(): lax.ppermute(value, 'seq', [(i, (i + distance) % size) for i in range(siz...  4.1 us
    pallas_call x1, Pallas kernels, run(): call(functools.partial(fresh_kernel, order, tok, heads), 'fresh', [SMEM]...  3.91 us
    unnamed x20, local copies, waits for them, and re-layouts  3.03 us
    pallas_call x1, Pallas kernels, run(): call(functools.partial(norm_kernel, order, heads), 'norm', [SMEM] + [VMEM...  3.02 us
    pallas_call x1, Pallas kernels, body(): call(functools.partial(compact_kernel, slots, tok, blocks), 'compact', [S...  3.01 us
  transfers between devices with their start and end apart: 15, of which 6 were waited for; matrix products, arithmetic and copies ran while one was open for 1% of the time, Pallas kernels for 13%

commit v1 on v0

v1 whole, which is shorter than its diff:
```python
import functools
import math

import jax
import jax.numpy as jnp
import numpy as np
from jax import lax
from jax.experimental import pallas as pl
from jax.experimental.pallas import tpu as pltpu
from jax.sharding import PartitionSpec as P

HEAD = 128
RMS_EPS = 1e-06
VMEM_BYTES = 32 * 1024 * 1024
TILE = 512
SMEM, VMEM = pltpu.SMEM, pltpu.VMEM


def call(kernel, name, ins, outs, flops, n_bytes, scratch=(), vmem_bytes=VMEM_BYTES):
    shapes = [jax.ShapeDtypeStruct(shape, dtype) for _, shape, dtype in outs]
    return pl.pallas_call(
        kernel,
        out_shape=shapes,
        in_specs=[pl.BlockSpec(memory_space=m) for m in ins],
        out_specs=[pl.BlockSpec(memory_space=m) for m, _, _ in outs],
        scratch_shapes=scratch,
        compiler_params=pltpu.CompilerParams(vmem_limit_bytes=vmem_bytes),
        cost_estimate=pl.CostEstimate(flops=flops, bytes_accessed=n_bytes, transcendentals=0),
        name=name,
    )


def to_partner(value, distance, size):
    if distance == 0:
        return value
    return lax.ppermute(value, "seq", [(i, i ^ distance) for i in range(size)])


def to_block(value, distance, size):
    return lax.ppermute(value, "seq", [(i, (i + distance) % size) for i in range(size)])


def column(h):
    return slice(h * HEAD, (h + 1) * HEAD)


def place(slots):
    device = lax.axis_index("seq")
    return lax.rem(device, slots), lax.div(device, slots)


def live_of(assign, counts, index):
    return counts[assign[index]]


def live_lanes(assign, counts, tok, indices):
    width = tok * len(indices)
    lane = lax.broadcasted_iota(jnp.int32, (1, width), 1)
    count = jnp.zeros((1, width), jnp.int32)
    for i, index in enumerate(indices):
        count = jnp.where(lane // tok == i, live_of(assign, counts, index), count)
    return lane % tok, count


def most_kernel(slots, blocks, assign, counts, out):
    most = jnp.int32(0)
    for b in range(blocks):
        total = jnp.int32(0)
        for i in range(slots):
            total = total + live_of(assign, counts, b * slots + i)
        most = jnp.maximum(most, total)
    out[0] = most


def compact_kernel(slots, tok, assign, counts, keys, values, out):
    rows, width, wide = out.shape[0], slots * tok, keys.shape[2]
    _, block = place(slots)
    indices = [block * slots + i for i in range(slots)]
    within, count = live_lanes(assign, counts, tok, indices)
    lane = lax.broadcasted_iota(jnp.int32, (1, width), 1)
    ahead = jnp.zeros((1, width), jnp.int32)
    for i, index in enumerate(indices):
        ahead = ahead + jnp.where(lane // tok > i, live_of(assign, counts, index), 0)
    goal = jnp.where(within < count, ahead + within, -1)
    row = lax.broadcasted_iota(jnp.int32, (rows, width), 0)
    pick = jnp.where(row == goal, 1.0, 0.0).astype(jnp.bfloat16)
    for part, ref in enumerate((keys, values)):
        moved = jnp.dot(pick, ref[0], preferred_element_type=jnp.float32)
        out[:, part * wide : (part + 1) * wide] = moved.astype(jnp.bfloat16)


def norm_kernel(order, heads, assign, q, k, v, q_gain, k_gain, steps, *outs):
    tok, width = q.shape
    slot, block = place(len(order))
    patch = assign[block * len(order) + slot]
    position = patch * tok + lax.broadcasted_iota(jnp.int32, (tok, HEAD), 0)
    angles = position.astype(jnp.float32) * steps[...]
    low = lax.broadcasted_iota(jnp.int32, (tok, HEAD), 1) < HEAD // 2
    cos_part = jnp.cos(angles)
    sin_part = jnp.sin(angles)
    sin_part = jnp.where(low, -sin_part, sin_part)

    def inverse(ref):
        total = jnp.zeros((tok, HEAD), jnp.float32)
        for c in range(0, width, HEAD):
            x = ref[:, c : c + HEAD].astype(jnp.float32)
            total = total + x * x
        return lax.rsqrt(jnp.sum(total, axis=1, keepdims=True) / width + RMS_EPS)

    scales = inverse(q), inverse(k)
    wide = heads * HEAD
    for out, d in zip(outs, order):
        cols = pl.ds(pl.multiple_of(jnp.bitwise_xor(slot, d) * wide, wide), wide)
        out[2 * tok : 3 * tok, :] = v[:, cols]
        for part, (ref, gain) in enumerate(((q, q_gain), (k, k_gain))):
            entries, gains = ref[:, cols], gain[:, cols]
            for h in range(heads):
                x = entries[:, column(h)].astype(jnp.float32) * scales[part]
                x = x * gains[:, column(h)].astype(jnp.float32)
                turned = x * cos_part + pltpu.roll(x, HEAD // 2, 1) * sin_part
                out[part * tok : (part + 1) * tok, column(h)] = turned.astype(jnp.bfloat16)


def cache_kernel(order, tok, *refs):
    new_keys, new_values = refs[len(order) :]
    slot, _ = place(len(order))
    for ref, d in zip(refs, order):
        at = pl.ds(pl.multiple_of(jnp.bitwise_xor(slot, d) * tok, tok), tok)
        new_keys[0, at, :] = ref[tok : 2 * tok, :]
        new_values[0, at, :] = ref[2 * tok : 3 * tok, :]


def attend(queries, sources, state):
    scale = HEAD**-0.5 / math.log(2.0)
    scores = [
        lax.dot_general(
            queries, keys, (((1,), (1,)), ((), ())), preferred_element_type=jnp.float32
        )
        + bias
        for keys, _, bias in sources
    ]
    tops = [jnp.max(s, axis=1, keepdims=True) for s in scores]
    top = functools.reduce(jnp.maximum, tops + ([] if state is None else [state[0]]))
    weights = [jnp.exp2(s * scale - top * scale) for s in scores]
    total = sum(jnp.sum(w, axis=1, keepdims=True) for w in weights)
    summed = sum(
        jnp.dot(w.astype(jnp.bfloat16), values, preferred_element_type=jnp.float32)
        for w, (_, values, _) in zip(weights, sources)
    )
    if state is not None:
        fading = jnp.exp2((state[0] - top) * scale)
        total = total + state[1] * fading
        summed = summed + state[2] * fading
    return top, total, summed


def store_state(stats, sums, at, parts):
    rows = parts[0][0].shape[0]
    lane = lax.broadcasted_iota(jnp.int32, (rows, HEAD), 1)
    packed = jnp.zeros((rows, HEAD), jnp.float32)
    for h, (top, total, summed) in enumerate(parts):
        packed = jnp.where(lane == h, top, packed)
        packed = jnp.where(lane == HEAD // 2 + h, total, packed)
        sums[at, column(h)] = summed
    stats[at, :] = packed


def load_state(stats, sums, at, h):
    half = HEAD // 2
    return stats[at, h : h + 1], stats[at, half + h : half + h + 1], sums[at, column(h)]


def attend_kernel(order, tok, blocks, heads, rows, step, n_state, assign, counts, *refs):
    slots = len(order)
    bundles, refs = refs[:slots], refs[slots:]
    stale, state, rest = refs[0], refs[1 : 1 + n_state], refs[1 + n_state :]
    final = step == blocks - 1
    slot, block = place(slots)
    source = lax.rem(block - step + blocks, blocks) * slots
    live = jnp.int32(0)
    for i in range(slots):
        live = live + live_of(assign, counts, source + i)
    lane = lax.broadcasted_iota(jnp.int32, (1, stale.shape[0]), 1)
    stale_bias = jnp.where(lane < live, 0.0, -jnp.inf)
    if final:
        rest[-(rows[1] - rows[0]) // tok - 1][...] = jnp.zeros((8, HEAD), jnp.float32)
        gate, outs = rest[0], rest[-(rows[1] - rows[0]) // tok :]
        indices = [block * slots + jnp.bitwise_xor(slot, d) for d in order]
        within, count = live_lanes(assign, counts, tok, indices)
        fresh_bias = jnp.where(within < count, 0.0, -jnp.inf)

    def fresh(part, first, last, cols):
        rows = [bundles[i][part * tok : (part + 1) * tok, cols] for i in range(first, last)]
        return jnp.concatenate(rows, axis=0)

    per_tile = min(TILE, rows[1] - rows[0]) // tok
    for first in range(rows[0] // tok, rows[1] // tok, per_tile):
        at = slice(first * tok, (first + per_tile) * tok)
        parts = []
        for h in range(heads):
            cols = column(h)
            sources = [(stale[:, cols], stale[:, column(heads + h)], stale_bias)]
            if final:
                keys, values = fresh(1, 0, slots, cols), fresh(2, 0, slots, cols)
                sources.append((keys, values, fresh_bias))
            before = load_state(*state, at, h) if state else None
            _, total, summed = result = attend(
                fresh(0, first, first + per_tile, cols), sources, before
            )
            parts.append(result)
            if final:
                rounded = (summed / total).astype(jnp.bfloat16).astype(jnp.float32)
                gated = (rounded * gate[:, cols].astype(jnp.float32)).astype(jnp.bfloat16)
                for i in range(per_tile):
                    to = first + i - rows[0] // tok
                    outs[to][:, cols] = gated[i * tok : (i + 1) * tok]
        if not final:
            store_state(*rest, at, parts)


def collect_kernel(order, heads, *refs):
    wide = heads * HEAD
    slot, _ = place(len(order))
    for ref, d in zip(refs, order):
        start = jnp.bitwise_xor(slot, d) * wide
        refs[-1][:, pl.ds(pl.multiple_of(start, wide), wide)] = ref[...]


def body(
    q_fresh,
    k_fresh,
    v_fresh,
    q_gain,
    k_gain,
    stale_keys,
    stale_values,
    gate_table,
    assign,
    counts,
    timestep,
):
    bf16, f32, i32 = jnp.bfloat16, jnp.float32, jnp.int32
    device = lax.axis_index("seq")
    size = lax.axis_size("seq")
    tok, model_width = q_fresh.shape
    block_rows, wide = stale_keys.shape[1:]
    slots = model_width // wide
    blocks = size // slots
    heads = wide // HEAD
    order = sorted(range(slots), key=lambda d: (-(d & ~1).bit_count(), -d))
    sizes = [block_rows * n // 32 for n in (26, 28, 32)] if blocks == 2 else [block_rows]

    (most,) = call(
        functools.partial(most_kernel, slots, blocks),
        "most",
        [SMEM] * 2,
        [(SMEM, (1,), i32)],
        0,
        8 * (block_rows * wide + tok * model_width),
    )(assign, counts)

    halves = np.arange(HEAD, dtype=np.float64) % (HEAD // 2)
    steps = jnp.asarray((10000.0 ** (-2.0 * halves / HEAD)).astype(np.float32)[None])

    def exchange(arrays, order):
        return [to_partner(a, d, size) for a, d in zip(arrays, order)]

    def run(rows, operands):
        assign, counts, keys, values, q, k, v, q_gain, k_gain, gate_table, timestep = operands
        (packed,) = call(
            functools.partial(compact_kernel, slots, tok),
            "compact",
            [SMEM] * 2 + [VMEM] * 2,
            [(VMEM, (rows, 2 * wide), bf16)],
            4 * rows * block_rows * wide,
            4 * (rows + block_rows) * wide,
        )(assign, counts, keys, values)
        stale = [to_block(packed, s * slots, size) for s in range(1, blocks)]
        bundles = call(
            functools.partial(norm_kernel, order, heads),
            "norm",
            [SMEM] + [VMEM] * 6,
            [(VMEM, (3 * tok, wide), bf16)] * slots,
            20 * tok * model_width,
            12 * tok * model_width,
        )(assign, q, k, v, q_gain[None], k_gain[None], steps)
        fresh = exchange(bundles, order)
        gate = lax.dynamic_slice(gate_table, (timestep[0], device % slots * wide), (1, wide))
        state, back = [], []

        def step(s, rows, outs, extra):
            given = [*fresh, stale[s - 1], *state, *extra]
            return call(
                functools.partial(
                    attend_kernel, order, tok, blocks, heads, rows, s, len(state)
                ),
                "attend",
                [SMEM] * 2 + [VMEM] * len(given),
                outs,
                8 * (rows[1] - rows[0]) * block_rows * wide,
                16 * block_rows * wide,
            )(assign, counts, *given)

        for s in range(1, blocks - 1):
            state = step(
                s, (0, block_rows), [(VMEM, (block_rows, n), f32) for n in (HEAD, wide)], []
            )
        extra, start = [gate], 0
        for n in (slots,):
            part = order[start : start + n]
            outs = [(VMEM, (8, HEAD), f32)] + [(VMEM, (tok, wide), bf16)] * n
            ends = (start * tok, (start + n) * tok)
            after, *outs = step(blocks - 1, ends, outs, extra)
            extra, start = [gate, after], start + n
            back += exchange(outs, part)
        new_keys, new_values = call(
            functools.partial(cache_kernel, order, tok),
            "cache",
            [VMEM] * slots,
            [(VMEM, (1, block_rows, wide), bf16)] * 2,
            0,
            8 * block_rows * wide,
        )(*fresh)
        (mixed,) = call(
            functools.partial(collect_kernel, order, heads),
            "collect",
            [VMEM] * len(back),
            [(VMEM, (tok, model_width), bf16)],
            0,
            4 * tok * model_width,
        )(*back)
        return mixed, new_keys, new_values

    operands = (
        assign,
        counts,
        stale_keys,
        stale_values,
        q_fresh,
        k_fresh,
        v_fresh,
        q_gain,
        k_gain,
        gate_table,
        timestep,
    )
    which = sum((most[0] > n).astype(i32) for n in sizes[:-1])
    return lax.switch(which, [functools.partial(run, rows) for rows in sizes], operands)


def solution(mesh):
    rows = P(("groups", "seq"), None)
    entries = P(("groups", "seq"), None, None)
    return jax.shard_map(
        body,
        mesh=mesh,
        in_specs=(
            rows,
            rows,
            rows,
            P(),
            P(),
            entries,
            entries,
            P(),
            P("groups"),
            P("groups"),
            P("groups"),
        ),
        out_specs=(rows, entries, entries),
        check_vma=False,
    )
```

time: 84.1 us -> 78.7 us (0.936)
  Pallas kernels: 17.2 us -> 12.8 us
  local copies, waits for them, and re-layouts: 3.85 us -> 1.7 us
  starting transfers between devices: 16.4 us -> 15.3 us
  waiting for transfers between devices: 42.7 us -> 43.8 us
    pallas_call x4 -> x3, Pallas kernels: 12.9 us -> 9.23 us  [the longest x1 5.71 us: step(): call(functools.partial(attend_kernel, order, tok, blocks, heads, rows, s,...]
    unnamed x20 -> x2, local copies, waits for them, and re-layouts: 3.03 us -> 0.83 us
    ppermute x14, starting transfers between devices: 12.3 us -> 11.2 us  [to_partner(): return lax.ppermute(value, 'seq', [(i, i ^ distance) for i in range(size)])]
    ppermute x14, waiting for transfers between devices: 42.7 us -> 43.8 us  [to_partner(): return lax.ppermute(value, 'seq', [(i, i ^ distance) for i in range(size)])]
  transfers between devices with their start and end apart: 15 -> 15, of which waited for: 6 -> 8; matrix products, arithmetic and copies ran while one was open for 1% -> 1% of each run, Pallas kernels for 13% -> 5%
where the time goes in v1:
time: 78.7 us; the launch traced here: 78.4 us
  waiting for transfers between devices  43.8 us (56%)
  starting transfers between devices  15.3 us (19%)
  Pallas kernels  12.8 us (16%)
  loops' own time  2.82 us (4%)
  between operations  1.96 us (2%)
  local copies, waits for them, and re-layouts  1.7 us (2%)
    ppermute x14, waiting for transfers between devices, to_partner(): return lax.ppermute(value, 'seq', [(i, i ^ distance) for i in range(size)])  43.8 us
    ppermute x14, starting transfers between devices, to_partner(): return lax.ppermute(value, 'seq', [(i, i ^ distance) for i in range(size)])  11.2 us
    pallas_call x1, Pallas kernels, step(): call(functools.partial(attend_kernel, order, tok, blocks, heads, rows, s,...  5.71 us
    ppermute x1, starting transfers between devices, to_block(): lax.ppermute(value, 'seq', [(i, (i + distance) % size) for i in range(siz...  4.1 us
    another operation x1, loops' own time, body(): lax.switch(which, [functools.partial(run, rows) for rows in sizes], opera...  2.82 us
    pallas_call x1, Pallas kernels, run(): call(functools.partial(norm_kernel, order, heads), 'norm', [SMEM] + [VMEM...  2.37 us
    pallas_call x1, Pallas kernels, run(): call(functools.partial(compact_kernel, slots, tok), 'compact', [SMEM] * 2...  2.31 us
  transfers between devices with their start and end apart: 15, of which 8 were waited for; matrix products, arithmetic and copies ran while one was open for 1% of the time, Pallas kernels for 5%

profile of v1, /device:TPU:0, one launch (start us, length us, event | category | flops | bytes accessed | tf_op | source)
XLA Modules:
  0.0 78.4 jit_solution(10413203699217595694)
XLA Ops:
  0.6 1.2 %most.1 = s32[1]{0:T(128)} custom-call(s32[16]{0:T(128)} %assign.1, s32[16]{0:T(128)} %counts.1), custom_call_target="tpu_custom_call" | custom-call | bytes 5242880 | tf_op jit(solution)/shard_map/most/pallas_call | solution.py:253
  3.1 74.4 %conditional.1 = (bf16[1,512,640]{2,1,0:T(8,128)(2,1)}, bf16[1,512,640]{2,1,0:T(8,128)(2,1)}, bf16[64,5120]{1,0:T(8,128)(2,1)S(1)}) conditional(s32[]{:T(128)} %bitcast.3, (bf16[5120]{0:T(1024)(128)(2,1)}, bf16[5120]{0:T(1024)(128)(2,1)}, s32[16]{0:T(128)}, bf16[64,5120]{1,0:T(8,128)(2,1)}, bf16[64,5120]{1,0:T(8,128)(2,1)}, ...), branch_computations={%region_0.1_spmd, %region_1.2_spmd, %region_2.3_spmd} | conditional | flops 2019819520 | bytes 38139912 | solution.py:348
  3.4 0.0 copy-start.11
  3.4 0.0 copy-start.4
  3.4 0.0 copy-start.7
  3.5 0.0 copy-start.23
  3.5 2.3 %compact.4 = bf16[448,1280]{1,0:T(8,128)(2,1)S(1)} custom-call(s32[16]{0:T(128)} %get-tuple-element.109.assign, s32[16]{0:T(128)} %get-tuple-element.110.counts, bf16[1,512,640]{2,1,0:T(8,128)(2,1)} %get-tuple-element.125.keys, bf16[1,512,640]{2,1,0:T(8,128)(2,1)} %get-tuple-element.126.values), custom_call_target="tpu_custom_call" | custom-call | flops 587202560 | bytes 2457600 | tf_op jit(solution)/shard_map/cond/branch_1_fun/compact/pallas_call | solution.py:270
  5.8 0.0 copy-start.20
  5.8 4.1 %collective-permute-start.22 = (bf16[448,1280]{1,0:T(8,128)(2,1)S(1)}, bf16[448,1280]{1,0:T(8,128)(2,1)}, u32[]{:S(2)}, u32[]{:S(2)}) collective-permute-start(bf16[448,1280]{1,0:T(8,128)(2,1)S(1)} %compact.4), channel_id=1, source_target_pairs={{0,8},{1,9},{2,10},{3,11},{4,12},{5,13},{6,14},{7,15},{8,0},{9,1},... | collective-permute-start | bytes 3440648 | tf_op jit(solution)/shard_map/cond/branch_1_fun/ppermute | solution.py:40
  10.0 2.4 %norm.4 = (bf16[192,640]{1,0:T(8,128)(2,1)S(1)}, bf16[192,640]{1,0:T(8,128)(2,1)S(1)}, bf16[192,640]{1,0:T(8,128)(2,1)S(1)}, bf16[192,640]{1,0:T(8,128)(2,1)}, b...) custom-call(s32[16]{0:T(128)S(1)} %copy-done.17, ...), custom_call_target="tpu_custom_call" | custom-call | flops 6553600 | bytes 3932160 | tf_op jit(solution)/shard_map/cond/branch_1_fun/norm/pallas_call | solution.py:279
  12.4 1.7 %collective-permute-start.15 = (bf16[192,640]{1,0:T(8,128)(2,1)S(1)}, bf16[192,640]{1,0:T(8,128)(2,1)S(1)}, u32[]{:S(2)}, u32[]{:S(2)}) collective-permute-start(bf16[192,640]{1,0:T(8,128)(2,1)S(1)} %get-tuple-element.117), channel_id=1, source_target_pairs={{0,7},{1,6},{2,5},{3,4},{4,3},{5,2},{6,1},{7,0},{8,15},{9,14},{10,... | collective-permute-start | bytes 737288 | tf_op jit(solution)/shard_map/cond/branch_1_fun/ppermute | solution.py:36
  14.0 0.9 %collective-permute-start.16 = (bf16[192,640]{1,0:T(8,128)(2,1)S(1)}, bf16[192,640]{1,0:T(8,128)(2,1)S(1)}, u32[]{:S(2)}, u32[]{:S(2)}) collective-permute-start(bf16[192,640]{1,0:T(8,128)(2,1)S(1)} %get-tuple-element.118), channel_id=1, source_target_pairs={{0,6},{1,7},{2,4},{3,5},{4,2},{5,3},{6,0},{7,1},{8,14},{9,15},{10,... | collective-permute-start | bytes 737288 | tf_op jit(solution)/shard_map/cond/branch_1_fun/ppermute | solution.py:36
  14.9 1.4 %collective-permute-start.17 = (bf16[192,640]{1,0:T(8,128)(2,1)S(1)}, bf16[192,640]{1,0:T(8,128)(2,1)S(1)}, u32[]{:S(2)}, u32[]{:S(2)}) collective-permute-start(bf16[192,640]{1,0:T(8,128)(2,1)S(1)} %get-tuple-element.119), channel_id=1, source_target_pairs={{0,5},{1,4},{2,7},{3,6},{4,1},{5,0},{6,3},{7,2},{8,13},{9,12},{10,... | collective-permute-start | bytes 737288 | tf_op jit(solution)/shard_map/cond/branch_1_fun/ppermute | solution.py:36
  16.3 0.4 collective-permute-start.18
  16.8 24.1 %collective-permute-done.15.refs_0_ = bf16[192,640]{1,0:T(8,128)(2,1)S(1)} collective-permute-done((bf16[192,640]{1,0:T(8,128)(2,1)S(1)}, bf16[192,640]{1,0:T(8,128)(2,1)S(1)}, u32[]{:S(2)}, u32[]{:S(2)}) %collective-permute-start.15) | collective-permute-done | bytes 245792 | tf_op jit(solution)/shard_map/cond/branch_1_fun/ppermute | solution.py:36
  40.9 5.3 %collective-permute-done.16.refs_1_ = bf16[192,640]{1,0:T(8,128)(2,1)S(1)} collective-permute-done((bf16[192,640]{1,0:T(8,128)(2,1)S(1)}, bf16[192,640]{1,0:T(8,128)(2,1)S(1)}, u32[]{:S(2)}, u32[]{:S(2)}) %collective-permute-start.16) | collective-permute-done | bytes 245792 | tf_op jit(solution)/shard_map/cond/branch_1_fun/ppermute | solution.py:36
  46.2 1.5 %collective-permute-start.20 = (bf16[192,640]{1,0:T(8,128)(2,1)}, bf16[192,640]{1,0:T(8,128)(2,1)S(1)}, u32[]{:S(2)}, u32[]{:S(2)}) collective-permute-start(bf16[192,640]{1,0:T(8,128)(2,1)} %get-tuple-element.122), channel_id=1, source_target_pairs={{0,2},{1,3},{2,0},{3,1},{4,6},{5,7},{6,4},{7,5},{8,10},{9,11},{10,... | collective-permute-start | bytes 737288 | tf_op jit(solution)/shard_map/cond/branch_1_fun/ppermute | solution.py:36
  47.7 3.8 %collective-permute-done.17.refs_2_ = bf16[192,640]{1,0:T(8,128)(2,1)S(1)} collective-permute-done((bf16[192,640]{1,0:T(8,128)(2,1)S(1)}, bf16[192,640]{1,0:T(8,128)(2,1)S(1)}, u32[]{:S(2)}, u32[]{:S(2)}) %collective-permute-start.17) | collective-permute-done | bytes 245792 | tf_op jit(solution)/shard_map/cond/branch_1_fun/ppermute | solution.py:36
  53.4 0.8 %dynamic_slice.7.refs_9_ = bf16[1,640]{1,0:T(2,128)(2,1)S(1)} dynamic-slice(bf16[50,5120]{1,0:T(8,128)(2,1)} %get-tuple-element.127, s32[]{:T(128)S(6)} %select_n.27, s32[]{:T(128)S(6)} %select_n.29), dynamic_slice_sizes={1,640} | dynamic-slice | bytes 2564 | tf_op jit(solution)/shard_map/cond/branch_1_fun/dynamic_slice | solution.py:288
  54.2 6.1 %collective-permute-done.18.refs_3_ = bf16[192,640]{1,0:T(8,128)(2,1)S(1)} collective-permute-done((bf16[192,640]{1,0:T(8,128)(2,1)}, bf16[192,640]{1,0:T(8,128)(2,1)S(1)}, u32[]{:S(2)}, u32[]{:S(2)}) %collective-permute-start.18) | collective-permute-done | bytes 245792 | tf_op jit(solution)/shard_map/cond/branch_1_fun/ppermute | solution.py:36
  60.3 5.7 %attend.4 = (f32[8,128]{1,0:T(8,128)}, bf16[64,640]{1,0:T(8,128)(2,1)S(1)}, bf16[64,640]{1,0:T(8,128)(2,1)S(1)}, bf16[64,640]{1,0:T(8,128)(2,1)S(1)}, bf16[64,64...) custom-call(s32[16]{0:T(128)S(1)} %copy-done.17, ...), custom_call_target="tpu_custom_call" | custom-call | flops 1342177280 | bytes 5242880 | tf_op jit(solution)/shard_map/cond/branch_1_fun/attend/pallas_call | solution.py:293
  66.0 0.7 collective-permute-start.23
  66.7 1.9 %collective-permute-start.24 = (bf16[64,640]{1,0:T(8,128)(2,1)S(1)}, bf16[64,640]{1,0:T(8,128)(2,1)S(1)}, u32[]{:S(2)}, u32[]{:S(2)}) collective-permute-start(bf16[64,640]{1,0:T(8,128)(2,1)S(1)} %get-tuple-element.131), channel_id=1, source_target_pairs={{0,6},{1,7},{2,4},{3,5},{4,2},{5,3},{6,0},{7,1},{8,14},{9,15},{10,... | collective-permute-start | bytes 245768 | tf_op jit(solution)/shard_map/cond/branch_1_fun/ppermute | solution.py:36
  68.7 1.7 %collective-permute-start.26 = (bf16[64,640]{1,0:T(8,128)(2,1)S(1)}, bf16[64,640]{1,0:T(8,128)(2,1)S(1)}, u32[]{:S(2)}, u32[]{:S(2)}) collective-permute-start(bf16[64,640]{1,0:T(8,128)(2,1)S(1)} %get-tuple-element.133), channel_id=1, source_target_pairs={{0,4},{1,5},{2,6},{3,7},{4,0},{5,1},{6,2},{7,3},{8,12},{9,13},{10,... | collective-permute-start | bytes 245768 | tf_op jit(solution)/shard_map/cond/branch_1_fun/ppermute | solution.py:36
  70.4 0.9 %collective-permute-done.23.refs_0_ = bf16[64,640]{1,0:T(8,128)(2,1)S(1)} collective-permute-done((bf16[64,640]{1,0:T(8,128)(2,1)S(1)}, bf16[64,640]{1,0:T(8,128)(2,1)S(1)}, u32[]{:S(2)}, u32[]{:S(2)}) %collective-permute-start.23) | collective-permute-done | bytes 81952 | tf_op jit(solution)/shard_map/cond/branch_1_fun/ppermute | solution.py:36
  71.3 0.9 %collective-permute-start.28 = (bf16[64,640]{1,0:T(8,128)(2,1)S(1)}, bf16[64,640]{1,0:T(8,128)(2,1)S(1)}, u32[]{:S(2)}, u32[]{:S(2)}) collective-permute-start(bf16[64,640]{1,0:T(8,128)(2,1)S(1)} %get-tuple-element.135), channel_id=1, source_target_pairs={{0,2},{1,3},{2,0},{3,1},{4,6},{5,7},{6,4},{7,5},{8,10},{9,11},{10,... | collective-permute-start | bytes 245768 | tf_op jit(solution)/shard_map/cond/branch_1_fun/ppermute | solution.py:36
  72.2 1.5 %collective-permute-done.24.refs_1_ = bf16[64,640]{1,0:T(8,128)(2,1)S(1)} collective-permute-done((bf16[64,640]{1,0:T(8,128)(2,1)S(1)}, bf16[64,640]{1,0:T(8,128)(2,1)S(1)}, u32[]{:S(2)}, u32[]{:S(2)}) %collective-permute-start.24) | collective-permute-done | bytes 81952 | tf_op jit(solution)/shard_map/cond/branch_1_fun/ppermute | solution.py:36
  73.7 1.2 %cache.4 = (bf16[1,512,640]{2,1,0:T(8,128)(2,1)}, bf16[1,512,640]{2,1,0:T(8,128)(2,1)}) custom-call(bf16[192,640]{1,0:T(8,128)(2,1)S(1)} %collective-permute-done.15.refs_0_, bf16[192,640]{1,0:T(8,128)(2,1)S(1)} %collective-permute-done.16.refs_1_, bf16[192,640]{1,0:T(8,128)(2,1)S(1)} %collective-permute-done.17.refs_2_, ...), custom_call_target="tpu_custom_call" | custom-call | bytes 2621440 | tf_op jit(solution)/shard_map/cond/branch_1_fun/cache/pallas_call | solution.py:316
  74.9 0.6 collective-permute-done.26.refs_3_
  75.5 1.6 %collective-permute-done.28.refs_5_ = bf16[64,640]{1,0:T(8,128)(2,1)S(1)} collective-permute-done((bf16[64,640]{1,0:T(8,128)(2,1)S(1)}, bf16[64,640]{1,0:T(8,128)(2,1)S(1)}, u32[]{:S(2)}, u32[]{:S(2)}) %collective-permute-start.28) | collective-permute-done | bytes 81952 | tf_op jit(solution)/shard_map/cond/branch_1_fun/ppermute | solution.py:36
  77.0 0.1 collect.4
  77.6 0.8 %copy-done.9 = bf16[64,5120]{1,0:T(8,128)(2,1)} copy-done((bf16[64,5120]{1,0:T(8,128)(2,1)}, bf16[64,5120]{1,0:T(8,128)(2,1)S(1)}, u32[]{:S(2)}) %copy-start.9) | copy-done | bytes 655384
  (26 shorter events, 0.1 us)
Async XLA Ops:
  3.4 6.5 %copy-start.11 = (bf16[5120]{0:T(1024)(128)(2,1)S(1)}, bf16[5120]{0:T(1024)(128)(2,1)}, u32[]{:S(2)}) copy-start(bf16[5120]{0:T(1024)(128)(2,1)} %get-tuple-element.114) | copy-start | bytes 30724 | tf_op jit(solution)/shard_map/cond
  3.4 6.5 %copy-start.14 = (bf16[5120]{0:T(1024)(128)(2,1)S(1)}, bf16[5120]{0:T(1024)(128)(2,1)}, u32[]{:S(2)}) copy-start(bf16[5120]{0:T(1024)(128)(2,1)} %get-tuple-element.115) | copy-start | bytes 30724 | tf_op jit(solution)/shard_map/cond
  3.4 6.5 %copy-start.1 = (bf16[64,5120]{1,0:T(8,128)(2,1)S(1)}, bf16[64,5120]{1,0:T(8,128)(2,1)}, u32[]{:S(2)}) copy-start(bf16[64,5120]{1,0:T(8,128)(2,1)} %get-tuple-element.111.q) | copy-start | bytes 1966084 | tf_op jit(solution)/shard_map/cond
  3.4 6.5 %copy-start.4 = (bf16[64,5120]{1,0:T(8,128)(2,1)S(1)}, bf16[64,5120]{1,0:T(8,128)(2,1)}, u32[]{:S(2)}) copy-start(bf16[64,5120]{1,0:T(8,128)(2,1)} %get-tuple-element.112.k) | copy-start | bytes 1966084 | tf_op jit(solution)/shard_map/cond
  3.4 6.5 %copy-start.7 = (bf16[64,5120]{1,0:T(8,128)(2,1)S(1)}, bf16[64,5120]{1,0:T(8,128)(2,1)}, u32[]{:S(2)}) copy-start(bf16[64,5120]{1,0:T(8,128)(2,1)} %get-tuple-element.113.v) | copy-start | bytes 1966084 | tf_op jit(solution)/shard_map/cond
  3.5 6.5 %copy-start.17 = (s32[16]{0:T(128)S(1)}, s32[16]{0:T(128)}, u32[]{:S(2)}) copy-start(s32[16]{0:T(128)} %get-tuple-element.109.assign) | copy-start | bytes 196 | tf_op jit(solution)/shard_map/cond
  3.5 6.5 %copy-start.23 = (f32[1,128]{1,0:T(1,128)S(1)}, f32[1,128]{1,0:T(1,128)}, u32[]{:S(2)}) copy-start(f32[1,128]{1,0:T(1,128)} %get-tuple-element.116.steps) | copy-start | bytes 1540 | tf_op jit(solution)/shard_map/cond
  5.8 54.5 %copy-start.20 = (s32[16]{0:T(128)S(1)}, s32[16]{0:T(128)}, u32[]{:S(2)}) copy-start(s32[16]{0:T(128)} %get-tuple-element.110.counts) | copy-start | bytes 196 | tf_op jit(solution)/shard_map/cond
  5.8 54.4 %collective-permute-start.22 = (bf16[448,1280]{1,0:T(8,128)(2,1)S(1)}, bf16[448,1280]{1,0:T(8,128)(2,1)}, u32[]{:S(2)}, u32[]{:S(2)}) collective-permute-start(bf16[448,1280]{1,0:T(8,128)(2,1)S(1)} %compact.4), channel_id=1, source_target_pairs={{0,8},{1,9},{2,10},{3,11},{4,12},{5,13},{6,14},{7,15},{8,0},{9,1},... | collective-permute-start | bytes 3440648 | tf_op jit(solution)/shard_map/cond/branch_1_fun/ppermute | solution.py:40
  12.4 28.5 %collective-permute-start.15 = (bf16[192,640]{1,0:T(8,128)(2,1)S(1)}, bf16[192,640]{1,0:T(8,128)(2,1)S(1)}, u32[]{:S(2)}, u32[]{:S(2)}) collective-permute-start(bf16[192,640]{1,0:T(8,128)(2,1)S(1)} %get-tuple-element.117), channel_id=1, source_target_pairs={{0,7},{1,6},{2,5},{3,4},{4,3},{5,2},{6,1},{7,0},{8,15},{9,14},{10,... | collective-permute-start | bytes 737288 | tf_op jit(solution)/shard_map/cond/branch_1_fun/ppermute | solution.py:36
  14.0 32.1 %collective-permute-start.16 = (bf16[192,640]{1,0:T(8,128)(2,1)S(1)}, bf16[192,640]{1,0:T(8,128)(2,1)S(1)}, u32[]{:S(2)}, u32[]{:S(2)}) collective-permute-start(bf16[192,640]{1,0:T(8,128)(2,1)S(1)} %get-tuple-element.118), channel_id=1, source_target_pairs={{0,6},{1,7},{2,4},{3,5},{4,2},{5,3},{6,0},{7,1},{8,14},{9,15},{10,... | collective-permute-start | bytes 737288 | tf_op jit(solution)/shard_map/cond/branch_1_fun/ppermute | solution.py:36
  14.9 36.5 %collective-permute-start.17 = (bf16[192,640]{1,0:T(8,128)(2,1)S(1)}, bf16[192,640]{1,0:T(8,128)(2,1)S(1)}, u32[]{:S(2)}, u32[]{:S(2)}) collective-permute-start(bf16[192,640]{1,0:T(8,128)(2,1)S(1)} %get-tuple-element.119), channel_id=1, source_target_pairs={{0,5},{1,4},{2,7},{3,6},{4,1},{5,0},{6,3},{7,2},{8,13},{9,12},{10,... | collective-permute-start | bytes 737288 | tf_op jit(solution)/shard_map/cond/branch_1_fun/ppermute | solution.py:36
  16.3 43.9 %collective-permute-start.18 = (bf16[192,640]{1,0:T(8,128)(2,1)}, bf16[192,640]{1,0:T(8,128)(2,1)S(1)}, u32[]{:S(2)}, u32[]{:S(2)}) collective-permute-start(bf16[192,640]{1,0:T(8,128)(2,1)} %get-tuple-element.120), channel_id=1, source_target_pairs={{0,4},{1,5},{2,6},{3,7},{4,0},{5,1},{6,2},{7,3},{8,12},{9,13},{10,... | collective-permute-start | bytes 737288 | tf_op jit(solution)/shard_map/cond/branch_1_fun/ppermute | solution.py:36
  40.9 19.4 %collective-permute-start.19 = (bf16[192,640]{1,0:T(8,128)(2,1)}, bf16[192,640]{1,0:T(8,128)(2,1)S(1)}, u32[]{:S(2)}, u32[]{:S(2)}) collective-permute-start(bf16[192,640]{1,0:T(8,128)(2,1)} %get-tuple-element.121), channel_id=1, source_target_pairs={{0,3},{1,2},{2,1},{3,0},{4,7},{5,6},{6,5},{7,4},{8,11},{9,10},{10,... | collective-permute-start | bytes 737288 | tf_op jit(solution)/shard_map/cond/branch_1_fun/ppermute | solution.py:36
  46.2 14.1 %collective-permute-start.20 = (bf16[192,640]{1,0:T(8,128)(2,1)}, bf16[192,640]{1,0:T(8,128)(2,1)S(1)}, u32[]{:S(2)}, u32[]{:S(2)}) collective-permute-start(bf16[192,640]{1,0:T(8,128)(2,1)} %get-tuple-element.122), channel_id=1, source_target_pairs={{0,2},{1,3},{2,0},{3,1},{4,6},{5,7},{6,4},{7,5},{8,10},{9,11},{10,... | collective-permute-start | bytes 737288 | tf_op jit(solution)/shard_map/cond/branch_1_fun/ppermute | solution.py:36
  51.4 8.8 %collective-permute-start.21 = (bf16[192,640]{1,0:T(8,128)(2,1)S(1)}, bf16[192,640]{1,0:T(8,128)(2,1)S(1)}, u32[]{:S(2)}, u32[]{:S(2)}) collective-permute-start(bf16[192,640]{1,0:T(8,128)(2,1)S(1)} %get-tuple-element.123), channel_id=1, source_target_pairs={{0,1},{1,0},{2,3},{3,2},{4,5},{5,4},{6,7},{7,6},{8,9},{9,8},{10,11... | collective-permute-start | bytes 737288 | tf_op jit(solution)/shard_map/cond/branch_1_fun/ppermute | solution.py:36
  66.0 5.3 %collective-permute-start.23 = (bf16[64,640]{1,0:T(8,128)(2,1)S(1)}, bf16[64,640]{1,0:T(8,128)(2,1)S(1)}, u32[]{:S(2)}, u32[]{:S(2)}) collective-permute-start(bf16[64,640]{1,0:T(8,128)(2,1)S(1)} %get-tuple-element.130), channel_id=1, source_target_pairs={{0,7},{1,6},{2,5},{3,4},{4,3},{5,2},{6,1},{7,0},{8,15},{9,14},{10,... | collective-permute-start | bytes 245768 | tf_op jit(solution)/shard_map/cond/branch_1_fun/ppermute | solution.py:36
  66.7 7.0 %collective-permute-start.24 = (bf16[64,640]{1,0:T(8,128)(2,1)S(1)}, bf16[64,640]{1,0:T(8,128)(2,1)S(1)}, u32[]{:S(2)}, u32[]{:S(2)}) collective-permute-start(bf16[64,640]{1,0:T(8,128)(2,1)S(1)} %get-tuple-element.131), channel_id=1, source_target_pairs={{0,6},{1,7},{2,4},{3,5},{4,2},{5,3},{6,0},{7,1},{8,14},{9,15},{10,... | collective-permute-start | bytes 245768 | tf_op jit(solution)/shard_map/cond/branch_1_fun/ppermute | solution.py:36
  68.7 6.2 %collective-permute-start.25 = (bf16[64,640]{1,0:T(8,128)(2,1)S(1)}, bf16[64,640]{1,0:T(8,128)(2,1)S(1)}, u32[]{:S(2)}, u32[]{:S(2)}) collective-permute-start(bf16[64,640]{1,0:T(8,128)(2,1)S(1)} %get-tuple-element.132), channel_id=1, source_target_pairs={{0,5},{1,4},{2,7},{3,6},{4,1},{5,0},{6,3},{7,2},{8,13},{9,12},{10,... | collective-permute-start | bytes 245768 | tf_op jit(solution)/shard_map/cond/branch_1_fun/ppermute | solution.py:36
  68.7 6.8 %collective-permute-start.26 = (bf16[64,640]{1,0:T(8,128)(2,1)S(1)}, bf16[64,640]{1,0:T(8,128)(2,1)S(1)}, u32[]{:S(2)}, u32[]{:S(2)}) collective-permute-start(bf16[64,640]{1,0:T(8,128)(2,1)S(1)} %get-tuple-element.133), channel_id=1, source_target_pairs={{0,4},{1,5},{2,6},{3,7},{4,0},{5,1},{6,2},{7,3},{8,12},{9,13},{10,... | collective-permute-start | bytes 245768 | tf_op jit(solution)/shard_map/cond/branch_1_fun/ppermute | solution.py:36
  70.4 5.1 %collective-permute-start.27 = (bf16[64,640]{1,0:T(8,128)(2,1)S(1)}, bf16[64,640]{1,0:T(8,128)(2,1)S(1)}, u32[]{:S(2)}, u32[]{:S(2)}) collective-permute-start(bf16[64,640]{1,0:T(8,128)(2,1)S(1)} %get-tuple-element.134), channel_id=1, source_target_pairs={{0,3},{1,2},{2,1},{3,0},{4,7},{5,6},{6,5},{7,4},{8,11},{9,10},{10,... | collective-permute-start | bytes 245768 | tf_op jit(solution)/shard_map/cond/branch_1_fun/ppermute | solution.py:36
  71.3 5.7 %collective-permute-start.28 = (bf16[64,640]{1,0:T(8,128)(2,1)S(1)}, bf16[64,640]{1,0:T(8,128)(2,1)S(1)}, u32[]{:S(2)}, u32[]{:S(2)}) collective-permute-start(bf16[64,640]{1,0:T(8,128)(2,1)S(1)} %get-tuple-element.135), channel_id=1, source_target_pairs={{0,2},{1,3},{2,0},{3,1},{4,6},{5,7},{6,4},{7,5},{8,10},{9,11},{10,... | collective-permute-start | bytes 245768 | tf_op jit(solution)/shard_map/cond/branch_1_fun/ppermute | solution.py:36
  73.7 3.4 %collective-permute-start.29 = (bf16[64,640]{1,0:T(8,128)(2,1)S(1)}, bf16[64,640]{1,0:T(8,128)(2,1)S(1)}, u32[]{:S(2)}, u32[]{:S(2)}) collective-permute-start(bf16[64,640]{1,0:T(8,128)(2,1)S(1)} %get-tuple-element.136), channel_id=1, source_target_pairs={{0,1},{1,0},{2,3},{3,2},{4,5},{5,4},{6,7},{7,6},{8,9},{9,8},{10,11... | collective-permute-start | bytes 245768 | tf_op jit(solution)/shard_map/cond/branch_1_fun/ppermute | solution.py:36
  77.6 0.8 %copy-start.9 = (bf16[64,5120]{1,0:T(8,128)(2,1)}, bf16[64,5120]{1,0:T(8,128)(2,1)S(1)}, u32[]{:S(2)}) copy-start(bf16[64,5120]{1,0:T(8,128)(2,1)S(1)} %get-tuple-element.174) | copy-start | bytes 1966084
